TPU v7x, 256 devices: a whole 4x4x8 slice. The times are simulated.
256 devices in a mesh: dp: 16 (over z, core), group: 16 (over x, y).
Axes of the slice: x: 4, y: 4, z: 8, core: 2. Of those that a mesh axis runs over, the one named last changes fastest.
Arguments:
- queries: bfloat16 [16, 16, 256, 1024], P('dp', 'group'), may hold values from -36 to 36
- resp_kv: bfloat16 [16, 16, 256, 256], P('dp', 'group'), may hold values from -4 to 4
- out_grad: bfloat16 [16, 16, 256, 1024], P('dp', 'group'), may hold values from -6 to 6
- prompt_key_value: bfloat16 [16, 2048, 256], P('dp', 'group'), may hold values from -12 to 12
- lengths: int32 [16, 16], P('dp', 'group'), may hold values from 1 to 256, 3072 in all within a row
- group_mask: int32 [16], P('dp'), may hold values from 0 to 1, as said below
Outputs:
- q_grad: bfloat16 [16, 16, 256, 1024], P('dp', 'group')
- response_key_value_gradient: bfloat16 [16, 16, 256, 256], P('dp', 'group')
- prompt_kv_grad: bfloat16 [16, 2048, 256], P('dp', 'group')
Inputs may be any that keep to these rules, and one draw needn't show every extreme that they name: The 16 lengths of each group sum to 3072, and the longest response of each group has exactly 256 tokens. `group_mask`: at least one group survives.
All inputs are finite; a program needn't handle non-finite values.
Results may differ from a plain program's by a relative error of at most 0.025.
Values may be sent and summed in bfloat16 or wider, within the bound.
A program may use at most 128 MiB of HBM per device.

v0:
```python
import jax
import jax.numpy as jnp
from jax import lax
from jax.sharding import PartitionSpec as P


def on_device(queries, resp_kv, out_grad, prompt_key_value, lengths, group_mask):
    resp_rows = queries.shape[2]
    head_width = resp_kv.shape[3] // 2
    head_count = queries.shape[3] // head_width
    members = lax.axis_size("group")
    groups = lax.axis_size("dp")
    prompt_all = lax.all_gather(prompt_key_value[0], "group", axis=0, tiled=True)
    prompt_len = prompt_all.shape[0]
    group_alive = group_mask[0]
    length = lengths[0, 0]
    token_total = lax.psum(group_alive * length, ("dp", "group"))
    factor = jnp.float32(groups * members * resp_rows) / token_total.astype(jnp.float32)
    inv_root = 1.0 / head_width**0.5
    all_keys = jnp.concatenate([prompt_all[:, :head_width], resp_kv[0, 0, :, :head_width]], 0)
    all_values = jnp.concatenate([prompt_all[:, head_width:], resp_kv[0, 0, :, head_width:]], 0)
    live_rows = (jnp.arange(resp_rows) < length) & (group_alive > 0)
    grad_in = jnp.where(live_rows[:, None], out_grad[0, 0], jnp.zeros_like(out_grad[0, 0]))
    query_rows = queries[0, 0].reshape(resp_rows, head_count, head_width)
    grad_rows = grad_in.reshape(resp_rows, head_count, head_width)
    column = jnp.arange(prompt_len + resp_rows)[None, :]
    row_index = jnp.arange(resp_rows)[:, None]
    allowed = (column < prompt_len) | (column - prompt_len <= row_index)
    kept_rows = prompt_len + resp_rows
    key_total = jnp.zeros((kept_rows, head_width), jnp.float32)
    value_total = jnp.zeros((kept_rows, head_width), jnp.float32)
    query_parts = []
    total_parts = []
    dot_parts = []
    for pair_start in range(0, head_count, 2):
        query_pair = query_rows[:, pair_start : pair_start + 2]
        grad_pair = grad_rows[:, pair_start : pair_start + 2]
        scores = (
            jnp.einsum("rhd,kd->hrk", query_pair, all_keys, preferred_element_type=jnp.float32)
            * inv_root
        )
        scores = jnp.where(allowed[None], scores, -jnp.inf)
        highest = jnp.max(scores, -1, keepdims=True)
        log_total = highest + jnp.log(jnp.sum(jnp.exp(scores - highest), -1, keepdims=True))
        attn_probs = jnp.exp(scores - log_total)
        probs_low = attn_probs.astype(jnp.bfloat16)
        attended = jnp.einsum(
            "hrk,kd->hrd", probs_low, all_values, preferred_element_type=jnp.float32
        )
        row_dots = jnp.sum(
            jnp.transpose(grad_pair, (1, 0, 2)).astype(jnp.float32) * attended, -1, keepdims=True
        )
        dprobs = jnp.einsum(
            "rhd,kd->hrk", grad_pair, all_values, preferred_element_type=jnp.float32
        )
        dscores = (attn_probs * (dprobs - row_dots)).astype(jnp.bfloat16)
        query_parts.append(
            jnp.einsum("hrk,kd->rhd", dscores, all_keys, preferred_element_type=jnp.float32)
            * inv_root
            * factor
        )
        key_total = key_total + jnp.einsum(
            "hrk,rhd->kd", dscores, query_pair, preferred_element_type=jnp.float32
        )
        value_total = value_total + jnp.einsum(
            "hrk,rhd->kd", probs_low, grad_pair, preferred_element_type=jnp.float32
        )
        total_parts.append(log_total)
        dot_parts.append(row_dots)
    query_grads = jnp.concatenate(query_parts, 1).reshape(resp_rows, head_count * head_width)
    kv_parts = jnp.concatenate([key_total * inv_root * factor, value_total * factor], 1)
    query_grads, kv_parts, log_totals, row_dots = (
        query_grads,
        kv_parts,
        jnp.concatenate(total_parts, 0),
        jnp.concatenate(dot_parts, 0),
    )
    resp_part = kv_parts[prompt_len:]
    prompt_share = lax.psum_scatter(
        kv_parts[:prompt_len].astype(jnp.bfloat16), "group", scatter_dimension=0, tiled=True
    )
    return (
        query_grads.astype(jnp.bfloat16).reshape(1, 1, resp_rows, head_count * head_width),
        resp_part.astype(jnp.bfloat16).reshape(1, 1, resp_rows, 2 * head_width),
        prompt_share[None],
    )


def solution(mesh):
    in_specs = (
        P("dp", "group", None, None),
        P("dp", "group", None, None),
        P("dp", "group", None, None),
        P("dp", "group", None),
        P("dp", "group"),
        P("dp"),
    )
    out_specs = (P("dp", "group", None, None), P("dp", "group", None, None), P("dp", "group", None))
    return jax.shard_map(
        on_device, mesh=mesh, in_specs=in_specs, out_specs=out_specs, check_vma=False
    )
```

profile of v0, /device:TPU:1, one launch (start us, length us, event | category | flops | bytes accessed | tf_op | source)
XLA Modules:
  0.0 203.8 jit_solution(8268860265511061419)
XLA Ops:
  9.2 81.6 %psum.7 = s32[]{:T(128)} all-reduce(s32[]{:T(128)S(6)} %mul.105), channel_id=1, replica_groups=mesh['dp'=16,'group'=16] {'dp','group'}, use_global_device_ids=true, to_apply=%region_3.4 | all-reduce | flops 1 | bytes 8 | tf_op jit(solution)/shard_map/psum | solution.py:17
  91.6 1.2 copy.94
  92.8 1.4 copy.96
  94.8 1.6 fusion.32
  96.4 1.3 fusion.71
  100.5 0.9 convolution_bitcast_fusion.6
  101.5 0.9 fusion.39
  102.4 0.9 fusion.40
  103.3 0.9 convolution_bitcast_fusion.5
  105.7 0.9 fusion.41
  106.6 0.9 convolution_bitcast_fusion.4
  108.4 1.0 fusion.17
  110.3 1.2 fusion.18
  112.9 1.0 fusion.19
  116.0 0.9 fusion.38
  116.9 1.0 fusion.16
  118.0 1.0 fusion.31
  119.4 0.9 fusion.27
  120.3 1.2 fusion.33
  121.5 2.3 %copy.184 = bf16[2048,256]{1,0:T(8,128)(2,1)} copy(bf16[2048,256]{0,1:T(8,128)(2,1)} %fusion.33) | data formatting | bytes 2097152
  124.3 1.1 copy-done.1
  127.9 1.0 copy.137
  129.7 65.6 %reduce-scatter.4.cloned.1.call-done = bf16[128,256]{1,0:T(8,128)(2,1)} async-done(((bf16[2048,256]{1,0:T(8,128)(2,1)}), bf16[128,256]{1,0:T(8,128)(2,1)}) %reduce-scatter.4.cloned.1.call-update) | async-done | bytes 65552
  195.3 0.9 copy.185
  (55 shorter events, 15.4 us)
Async XLA Ops:
  7.2 87.5 %copy-start.10 = (bf16[1,1,256,256]{3,2,1,0:T(8,128)(2,1)S(1)}, bf16[1,1,256,256]{3,2,1,0:T(8,128)(2,1)}, u32[]{:S(2)}) copy-start(bf16[1,1,256,256]{3,2,1,0:T(8,128)(2,1)} %param.7) | copy-start | bytes 393220
  7.2 89.2 %all-gather.3.cloned.1.call-start = ((), (), s32[]{:S(2)}) async-start(), calls=%async_computation.1 | async-start | bytes 1114112 | tf_op jit(solution)/shard_map/all_gather | solution.py:13
  7.9 187.4 %reduce-scatter.4.cloned.1.call-start = ((), (), s32[]{:S(2)}) async-start(), calls=%async_computation.2 | async-start | bytes 1114112
  92.8 14.8 %copy-start.8 = (bf16[1,1,256,1024]{2,3,1,0:T(8,128)(2,1)}, bf16[1,1,256,1024]{2,3,1,0:T(8,128)(2,1)S(1)}, u32[]{:S(2)}) copy-start(bf16[1,1,256,1024]{2,3,1,0:T(8,128)(2,1)S(1)} %copy.94) | copy-start | bytes 1572868
  108.3 1.0 copy-start.9
  111.5 1.4 copy-start
  113.9 1.4 copy-start.2
  118.0 1.4 copy-start.4
  119.4 0.9 copy-start.6
  123.8 1.7 copy-start.1
  123.8 2.4 %copy-start.3 = (bf16[2,256,2304]{1,2,0:T(8,128)(2,1)S(1)}, bf16[2,256,2304]{1,2,0:T(8,128)(2,1)}, u32[]{:S(2)}) copy-start(bf16[2,256,2304]{1,2,0:T(8,128)(2,1)} %copy-done.2) | copy-start | bytes 7077892
  125.5 1.8 copy-start.5
  127.3 1.6 copy-start.7
Sparse Core Ops, SparseCore 0:
  10.4 50.0 all-gather.2
  123.9 71.3 reduce-scatter.3
where the time goes:
time: 205 us; the launch traced here: 204 us
  blocking collectives  81.6 us (40%)
  waiting for transfers between devices  66.3 us (32%)
  matrix products  20.5 us (10%)
  between operations  16.4 us (8%)
  local copies, waits for them, and re-layouts  13.3 us (6%)
  other arithmetic  5.57 us (3%)
    psum x1, blocking collectives, on_device(): token_total = lax.psum(group_alive * length, ('dp', 'group'))  81.6 us
    unnamed x3, waiting for transfers between devices  66.3 us
    unnamed x29, local copies, waits for them, and re-layouts  11.8 us
    dot_general x4, matrix products, on_device(): jnp.einsum('rhd,kd->hrk', grad_pair, all_values, preferred_element_type=j...  4.28 us
  transfers between devices with their start and end apart: 2, of which 1 were waited for; matrix products, arithmetic and copies ran while one was open for 4% of the time, Pallas kernels for 0%

commit v1 on v0

v1 whole, which is shorter than its diff:
```python
import functools
import math

import jax
import jax.numpy as jnp
from jax import lax
from jax.experimental import pallas as pl
from jax.experimental.pallas import tpu as pltpu
from jax.sharding import PartitionSpec as P

F32, BF16 = jnp.float32, jnp.bfloat16
MESH = pl.DeviceIdType.MESH
SIDE = 4
BLOCK = 128
CHUNK = 2 * BLOCK
LOWEST = -1e30
SUB = 64
SUBS = CHUNK // SUB

ORDER = [(1, 0), (0, 0), (0, 1), (2, 0), (0, 3), (3, 0), (3, 3), (1, 1),
         (2, 3), (1, 3), (0, 2), (2, 1), (3, 1), (3, 2), (1, 2), (2, 2)]
SLOT = {off: i + 2 for i, off in enumerate(ORDER)}
PLACE = {off: i for i, off in enumerate(off for off in ORDER if off != (0, 0))}
CHUNKS = (len(ORDER) + 2) // 2


def shifted(off, way):
    return ((off[0] - way[0]) % SIDE, (off[1] - way[1]) % SIDE)


GATHER = [((0, 0), (far, 0)) for far in (1, -1, 2)]
for i in (1, 0, 3, 2):
    way = 1 if i % 2 == 0 else -1
    GATHER += [((i, 0), (0, way)), ((i, 0), (0, -way)), ((i, -way % SIDE), (0, way))]
LANDS = {shifted(*move): move for move in GATHER}
REDUCE = {to: tuple(step if step == 2 else -step for step in way) for to, (_, way) in LANDS.items()}
TERMS = {off: [o for o in ORDER if o in REDUCE and shifted(o, REDUCE[o]) == off] for off in ORDER}

ARRIVALS = [[], [(3, 0), (1, 0)], [(0, 1), (2, 0)], [(3, 1), (0, 3)], [(3, 3), (1, 1)], [(2, 3), (1, 3)], [(0, 2), (2, 1)],
            [(1, 2), (3, 2)], [(2, 2)]]
DEPARTURES = [[(2, 2), (1, 2)], [(3, 2)], [(2, 1), (0, 2)], [(1, 3), (2, 3)], [(3, 1), (1, 1), (3, 3)], [(0, 3)],
              [(2, 0), (0, 1)], [(3, 0), (1, 0)], []]


def dot(a, b):
    return jnp.dot(a, b, preferred_element_type=F32)


def kernel(dp, heads, rows, scale, q_hbm, rkv_hbm, g_hbm, pkv_hbm, len_ref, mask_ref,
           q_out, r_out, p_out,
           q_ref, qs_ref, graw_ref, gs_ref, qt_ref, gt_ref, kv_ref, kt_ref, p_ref, dp_ref, m_ref, l_ref, d_ref, mh_ref,
           mf_ref, il_ref, rd_ref, dq_ref, part_ref, landed_ref, ak_ref, av_ref, mbuf, fac_ref,
           local_sem, ag_send, ag_recv, rs_send, rs_recv, mask_send, mask_recv):
    me_dp, me = lax.axis_index("dp"), lax.axis_index("group")
    core = me_dp % 2
    strides = (1 + core * (SIDE - 1), SIDE - core * (SIDE - 1))
    places = (me // strides[0] % SIDE, me // strides[1] % SIDE)

    def away(way):
        steps = [(place + step + SIDE) % SIDE - place for place, step in zip(places, way)]
        return (me_dp, me + steps[0] * strides[0] + steps[1] * strides[1])

    near = {way: away(way) for way in dict.fromkeys([w for _, w in GATHER] + list(REDUCE.values()))}
    sibling = (me_dp // 2 * 2 + (1 - me_dp % 2), me)
    above, below = ((me_dp + 2) % dp, me), ((me_dp + dp - 2) % dp, me)
    c2 = scale * math.log2(math.e)

    floor, ring = me_dp // 2, dp // 2
    mbuf[...] = jnp.zeros_like(mbuf)
    barrier = pltpu.get_barrier_semaphore()
    greeted = [*near.values(), sibling]
    for where in greeted:
        pl.semaphore_signal(barrier, inc=1, device_id=where, device_id_type=MESH)

    @pl.when((core == 1) & (floor < ring - 1))
    def _():
        pl.semaphore_signal(barrier, inc=1, device_id=above, device_id_type=MESH)

    @pl.when((core == 1) & (floor > 0))
    def _():
        pl.semaphore_signal(barrier, inc=1, device_id=below, device_id_type=MESH)

    ins = [
        pltpu.make_async_copy(pkv_hbm.at[0], kv_ref.at[pl.ds(SLOT[(0, 0)] * BLOCK, BLOCK)], local_sem.at[0]),
        pltpu.make_async_copy(q_hbm.at[0, 0], q_ref, local_sem.at[1]),
        pltpu.make_async_copy(g_hbm.at[0, 0], graw_ref, local_sem.at[2]),
        pltpu.make_async_copy(rkv_hbm.at[0, 0], kv_ref.at[pl.ds(0, rows)], local_sem.at[3]),
    ]
    for copy in ins:
        copy.start()

    at_end = (floor == 0) | (floor == ring - 1)

    @pl.when((core == 1) & at_end)
    def _():
        pl.semaphore_wait(barrier, len(greeted) + 1)

    @pl.when((core == 1) & jnp.logical_not(at_end))
    def _():
        pl.semaphore_wait(barrier, len(greeted) + 2)

    @pl.when(core == 0)
    def _():
        pl.semaphore_wait(barrier, len(greeted))


    def ag_copy(move):
        off, way = move
        to = shifted(off, way)
        return pltpu.make_async_remote_copy(
            src_ref=kv_ref.at[pl.ds(SLOT[off] * BLOCK, BLOCK)],
            dst_ref=kv_ref.at[pl.ds(SLOT[to] * BLOCK, BLOCK)],
            send_sem=ag_send.at[PLACE[to]],
            recv_sem=ag_recv.at[PLACE[to]],
            device_id=near[way],
            device_id_type=MESH,
        )

    def pass_on(off):
        for move in GATHER:
            if move[0] == off:
                ag_copy(move).start()

    def arrive(off):
        ag_copy(LANDS[off]).wait_recv()
        pass_on(off)

    ins[0].wait()
    pass_on((0, 0))

    most = ring - 1
    every = 3 + 2 * most

    def mask_copy(src, dst, where):
        return pltpu.make_async_remote_copy(
            src_ref=mbuf.at[src],
            dst_ref=mbuf.at[dst],
            send_sem=mask_send.at[dst],
            recv_sem=mask_recv.at[dst],
            device_id=where,
            device_id_type=MESH,
        )

    to_sibling = mask_copy(0, 1, sibling)
    total_back = mask_copy(every, every, sibling)
    lines = [
        ([mask_copy(2 if i == 0 else 2 + i, 3 + i, above) for i in range(most)], floor, most - floor),
        ([mask_copy(2 if i == 0 else 2 + most + i, 3 + most + i, below) for i in range(most)], most - floor, floor),
    ]

    def mask_step(i):
        if i == 0:
            to_sibling.wait_recv()
            mbuf[2] = mbuf[0] + mbuf[1]
        for copies, behind, ahead in lines:
            if i > 0:
                @pl.when(behind >= i)
                def _():
                    copies[i - 1].wait_recv()

            if i < most:
                @pl.when((behind >= i) & (ahead > 0))
                def _():
                    copies[i].start()
        if i == most:
            count = mbuf[2]
            for j in range(2 * most):
                count = count + mbuf[3 + j]
            mbuf[every] = count
            total_back.start()

    mbuf[0] = jnp.broadcast_to(mask_ref[...].astype(F32), (8, 128))

    @pl.when(core == 0)
    def _():
        to_sibling.start()

    m_ref[...] = jnp.full_like(m_ref, LOWEST)
    l_ref[...] = jnp.zeros_like(l_ref)
    d_ref[...] = jnp.zeros_like(d_ref)
    dq_ref[...] = jnp.zeros_like(dq_ref)
    ins[1].wait()
    for h in range(heads):
        q_h = q_ref[:, h * BLOCK : (h + 1) * BLOCK]
        qs_ref[h * rows : (h + 1) * rows, :] = q_h
        qt_ref[h] = q_h.T
    ins[2].wait()
    live = (lax.broadcasted_iota(jnp.int32, (rows, BLOCK), 0) < len_ref[...] * mask_ref[...]).astype(F32)
    for h in range(heads):
        masked = (graw_ref[:, h * BLOCK : (h + 1) * BLOCK].astype(F32) * live).astype(BF16)
        gs_ref[h * rows : (h + 1) * rows, :] = masked
        gt_ref[h] = masked.T
    ins[3].wait()

    def forward_head(c, h, keys, values, allowed):
        s = dot(keys, qt_ref[h])
        if allowed is not None:
            s = jnp.where(allowed, s, LOWEST)
        dprob = dot(values, gt_ref[h])
        dp_ref[c, h] = dprob
        stats = []
        for i in range(SUBS):
            span = slice(i * SUB, (i + 1) * SUB)
            s_i = s[span].reshape(SUB // 8, 8, rows)
            top = jnp.max(s_i, axis=0)
            p = jnp.exp2((s_i - top[None]) * c2)
            total = jnp.sum(p, axis=0)
            weighted = jnp.sum(p * dprob[span].reshape(p.shape), axis=0)
            mh_ref[c, h, i] = top
            p_ref[c, h, span, :] = p.reshape(SUB, rows).astype(BF16)
            stats.append((top, total, weighted))
        m_old = m_ref[h]
        m_new = functools.reduce(jnp.maximum, [top for top, _, _ in stats], m_old)
        fade = jnp.exp2((m_old - m_new) * c2)
        l_new, d_new = l_ref[h] * fade, d_ref[h] * fade
        for top, total, weighted in stats:
            fade = jnp.exp2((top - m_new) * c2)
            l_new, d_new = l_new + total * fade, d_new + weighted * fade
        m_ref[h], l_ref[h], d_ref[h] = m_new, l_new, d_new

    def chunk_kv(c):
        span = pl.ds(pl.multiple_of(c * CHUNK, CHUNK), CHUNK)
        keys, values = kv_ref[span, 0:BLOCK], kv_ref[span, BLOCK : 2 * BLOCK]
        kt_ref[c] = keys.T
        return keys, values

    for off in ARRIVALS[0]:
        arrive(off)

    keys0, values0 = chunk_kv(0)
    allowed = lax.broadcasted_iota(jnp.int32, (CHUNK, rows), 0) <= lax.broadcasted_iota(jnp.int32, (CHUNK, rows), 1)
    for h in range(heads):
        forward_head(0, h, keys0, values0, allowed)

    @pl.loop(1, CHUNKS)
    def _(c):
        for chunk in range(1, CHUNKS):
            @pl.when(c == chunk)
            def _():
                for off in ARRIVALS[chunk]:
                    arrive(off)

        for i in range(4):
            @pl.when((c == 2 * i + 1) & (core == 1))
            def _():
                mask_step(i)

        keys, values = chunk_kv(c)
        for h in range(heads):
            forward_head(c, h, keys, values, None)

    for h in range(heads):
        m = m_ref[h]
        top = jnp.max(m, axis=0, keepdims=True)
        w = jnp.exp2((m - top) * c2)
        inverse = 1.0 / jnp.sum(l_ref[h] * w, axis=0, keepdims=True)
        weighted = jnp.sum(d_ref[h] * w, axis=0, keepdims=True)
        mf_ref[h] = jnp.broadcast_to(top, (8, rows))
        il_ref[h] = jnp.broadcast_to(inverse, (8, rows))
        rd_ref[h] = jnp.broadcast_to(weighted * inverse, (8, rows))

    def rs_copy(off):
        return pltpu.make_async_remote_copy(
            src_ref=part_ref.at[pl.ds(SLOT[off] * BLOCK, BLOCK)],
            dst_ref=landed_ref.at[PLACE[off]],
            send_sem=rs_send.at[PLACE[off]],
            recv_sem=rs_recv.at[PLACE[off]],
            device_id=near[REDUCE[off]],
            device_id_type=MESH,
        )

    def summed(off):
        for o in TERMS[off]:
            rs_copy(o).wait_recv()
        total = part_ref[pl.ds(SLOT[off] * BLOCK, BLOCK), :].astype(F32)
        for o in TERMS[off]:
            total = total + landed_ref[PLACE[o]].astype(F32)
        return total

    def depart(off):
        if TERMS[off]:
            part_ref[pl.ds(SLOT[off] * BLOCK, BLOCK), :] = summed(off).astype(BF16)
        rs_copy(off).start()

    @pl.loop(0, CHUNKS)
    def _(step):
        c = CHUNKS - 1 - step
        k_total = jnp.zeros((CHUNK, BLOCK), F32)
        v_total = jnp.zeros((CHUNK, BLOCK), F32)
        for pair in range(0, heads, 2):
            probs2, dscores2 = [], []
            for h in (pair, pair + 1):
                probs, dscores = [], []
                inverse, row_dots = il_ref[h], rd_ref[h]
                for i in range(SUBS):
                    span = slice(i * SUB, (i + 1) * SUB)
                    share = jnp.exp2((mh_ref[c, h, i] - mf_ref[h]) * c2) * inverse
                    p = p_ref[c, h, span, :].astype(F32).reshape(SUB // 8, 8, rows) * share[None]
                    ds = p * (dp_ref[c, h, span, :].reshape(p.shape) - row_dots[None])
                    probs.append(p.reshape(SUB, rows).astype(BF16))
                    dscores.append(ds.reshape(SUB, rows).astype(BF16))
                probs2.append(jnp.concatenate(probs, axis=0))
                dscores2.append(jnp.concatenate(dscores, axis=0))
                dq_ref[h] = dq_ref[h] + dot(kt_ref[c], dscores2[-1])
            both = slice(pair * rows, (pair + 2) * rows)
            v_total = v_total + dot(jnp.concatenate(probs2, axis=1), gs_ref[both, :])
            k_total = k_total + dot(jnp.concatenate(dscores2, axis=1), qs_ref[both, :])
        ak_ref[...] = k_total
        av_ref[...] = v_total
        span = pl.ds(pl.multiple_of(c * CHUNK, CHUNK), CHUNK)
        part_ref[span, 0:BLOCK] = k_total.astype(BF16)
        part_ref[span, BLOCK : 2 * BLOCK] = v_total.astype(BF16)
        for i in range(4, most + 1):
            @pl.when((step == 2 * (i - 4)) & (core == 1))
            def _():
                mask_step(i)

        for at in range(CHUNKS):
            if DEPARTURES[at]:
                @pl.when(step == at)
                def _():
                    for off in DEPARTURES[at]:
                        depart(off)

    @pl.when(core == 0)
    def _():
        total_back.wait_recv()

    factor = 65536.0 / (mbuf[every] * 3072.0)
    fac_ref[...] = factor
    factor = fac_ref[0:1, :]
    factor_root = factor * scale
    r_out[0, 0, :, 0:BLOCK] = (ak_ref[...] * factor_root).astype(BF16)
    r_out[0, 0, :, BLOCK : 2 * BLOCK] = (av_ref[...] * factor).astype(BF16)
    for h in range(heads):
        q_out[0, 0, :, h * BLOCK : (h + 1) * BLOCK] = (dq_ref[h].T * factor_root).astype(BF16)
    for move in GATHER:
        ag_copy(move).wait_send()
    for off in REDUCE:
        if off not in DEPARTURES[-2]:
            rs_copy(off).wait_send()

    @pl.when(core == 0)
    def _():
        to_sibling.wait_send()

    @pl.when(core == 1)
    def _():
        total_back.wait_send()
        for copies, behind, ahead in lines:
            for i in range(most):
                @pl.when((behind >= i) & (ahead > 0))
                def _():
                    copies[i].wait_send()

    total = summed((0, 0))
    p_out[0, :, 0:BLOCK] = (total[:, 0:BLOCK] * factor_root).astype(BF16)
    p_out[0, :, BLOCK : 2 * BLOCK] = (total[:, BLOCK : 2 * BLOCK] * factor).astype(BF16)
    for off in DEPARTURES[-2]:
        rs_copy(off).wait_send()


def hand_over(*refs):
    count = (len(refs) - 1) // 2
    copies = []
    for src, dst in zip(refs[:count], refs[count:-1]):
        for at in range(0, src.shape[-2], 128):
            place = (*(0,) * (len(src.shape) - 2), pl.ds(at, 128))
            copies.append(pltpu.make_async_copy(src.at[place], dst.at[place], refs[-1].at[len(copies)]))
    for copy in copies:
        copy.start()
    for copy in copies:
        copy.wait()


def on_device(dp, queries, resp_kv, out_grad, prompt_key_value, lengths, group_mask):
    rows = queries.shape[2]
    heads = queries.shape[3] // BLOCK
    keys = CHUNKS * CHUNK
    vmem, sems = pltpu.VMEM, pltpu.SemaphoreType.DMA
    stat = vmem((heads, 8, rows), F32)
    shapes = tuple(jax.ShapeDtypeStruct(a.shape, BF16) for a in (queries, resp_kv, prompt_key_value))
    results = pl.pallas_call(
        functools.partial(kernel, dp, heads, rows, 1.0 / BLOCK**0.5),
        out_shape=tuple(pltpu.VMEM(a.shape, BF16) for a in shapes),
        in_specs=[pl.BlockSpec(memory_space=pl.ANY)] * 4 + [pl.BlockSpec(memory_space=pltpu.VMEM)] * 2,
        out_specs=[pl.BlockSpec(memory_space=pltpu.VMEM)] * 3,
        scratch_shapes=[
            vmem((rows, heads * BLOCK), BF16),
            vmem((heads * rows, BLOCK), BF16),
            vmem((rows, heads * BLOCK), BF16),
            vmem((heads * rows, BLOCK), BF16),
            vmem((heads, BLOCK, rows), BF16),
            vmem((heads, BLOCK, rows), BF16),
            vmem((keys, 2 * BLOCK), BF16),
            vmem((CHUNKS, BLOCK, CHUNK), BF16),
            vmem((CHUNKS, heads, CHUNK, rows), BF16),
            vmem((CHUNKS, heads, CHUNK, rows), F32),
            stat,
            stat,
            stat,
            vmem((CHUNKS, heads, SUBS, 8, rows), F32),
            stat,
            stat,
            stat,
            vmem((heads, BLOCK, rows), F32),
            vmem((keys, 2 * BLOCK), BF16),
            vmem((len(ORDER) - 1, BLOCK, 2 * BLOCK), BF16),
            vmem((CHUNK, BLOCK), F32),
            vmem((CHUNK, BLOCK), F32),
            vmem((dp + 2, 8, 128), F32),
            vmem((8, 128), F32),
            sems((4,)),
            sems((len(ORDER) - 1,)),
            sems((len(ORDER) - 1,)),
            sems((len(ORDER) - 1,)),
            sems((len(ORDER) - 1,)),
            sems((dp + 2,)),
            sems((dp + 2,)),
        ],
        compiler_params=pltpu.CompilerParams(
            collective_id=0, has_side_effects=True, vmem_limit_bytes=58 * 1024 * 1024
        ),
    )(queries, resp_kv, out_grad, prompt_key_value, lengths, group_mask.reshape(1, 1))
    return pl.pallas_call(
        hand_over,
        out_shape=shapes,
        in_specs=[pl.BlockSpec(memory_space=pltpu.VMEM)] * 3,
        out_specs=[pl.BlockSpec(memory_space=pl.ANY)] * 3,
        scratch_shapes=[sems((8,))],
        compiler_params=pltpu.CompilerParams(vmem_limit_bytes=1024 * 1024),
    )(*results)


def solution(mesh):
    in_specs = (
        P("dp", "group", None, None),
        P("dp", "group", None, None),
        P("dp", "group", None, None),
        P("dp", "group", None),
        P("dp", "group"),
        P("dp"),
    )
    out_specs = (P("dp", "group", None, None), P("dp", "group", None, None), P("dp", "group", None))
    return jax.shard_map(
        functools.partial(on_device, mesh.shape["dp"]), mesh=mesh, in_specs=in_specs, out_specs=out_specs, check_vma=False
    )
```

time: 205 us -> 37.6 us (0.18)
  blocking collectives: 81.6 us -> 0 us
  waiting for transfers between devices: 66.3 us -> 0 us
  Pallas kernels: 0 us -> 35.5 us
  matrix products: 20.5 us -> 0 us
  between operations: 16.4 us -> 1.93 us
  local copies, waits for them, and re-layouts: 13.3 us -> 0 us
  other arithmetic: 5.57 us -> 0 us
    psum x1 -> x0, blocking collectives: 81.6 us -> none  [on_device(): token_total = lax.psum(group_alive * length, ('dp', 'group'))]
    unnamed x3 -> x0, waiting for transfers between devices: 66.3 us -> none
    pallas_call x0 -> x2, Pallas kernels: none -> 35.5 us  [the longest x1 34.6 us: on_device(): pl.pallas_call(functools.partial(kernel, dp, heads, rows, 1.0 / BLOCK **...]
    dot_general x24 -> x0, matrix products: 20.5 us -> none  [the longest x4 4.28 us: on_device(): jnp.einsum('rhd,kd->hrk', grad_pair, all_values, preferred_element_type=j...]
    unnamed x29 -> x0, local copies, waits for them, and re-layouts: 11.8 us -> none
    reduce_sum x4 -> x0, other arithmetic: 2.54 us -> none  [on_device(): jnp.sum(jnp.exp(scores - highest), -1, keepdims=True)]
  transfers between devices with their start and end apart: 2 -> 0, of which waited for: 1 -> 0; matrix products, arithmetic and copies ran while one was open for 4% -> 0% of each run, Pallas kernels for 0% -> 0%
where the time goes in v1:
time: 37.6 us; the launch traced here: 37.4 us
  Pallas kernels  35.5 us (94%)
  between operations  1.93 us (5%)
    pallas_call x1, Pallas kernels, on_device(): pl.pallas_call(functools.partial(kernel, dp, heads, rows, 1.0 / BLOCK **...  34.6 us
    pallas_call x1, Pallas kernels, on_device(): pl.pallas_call(hand_over, out_shape=shapes, in_specs=[pl.BlockSpec(memory...  0.92 us

profile of v1, /device:TPU:1, one launch (start us, length us, event | category | flops | bytes accessed | tf_op | source)
XLA Modules:
  0.0 37.4 jit_solution(9366158586025058504)
XLA Ops:
  1.9 34.6 %shard_map.85 = (bf16[1,1,256,1024]{3,2,1,0:T(8,128)(2,1)S(1)}, bf16[1,1,256,256]{3,2,1,0:T(8,128)(2,1)S(1)}, bf16[1,128,256]{2,1,0:T(8,128)(2,1)S(1)}) custom-call(bf16[1,1,256,1024]{3,2,1,0:T(8,128)(2,1)} %q_hbm.1, bf16[1,1,256,256]{3,2,1,0:T(8,128)(2,1)} %rkv_hbm.1, bf16[1,1,256,1024]{3,2,1,0:T(8,128)(2,1)} %g_hbm.1, bf16[1,128,256]{2,1,0:T(8,128)(2,1)} %pkv_hbm.1, ...), custom_call_target="tpu_custom_call" | custom-call | tf_op jit(solution)/shard_map/pallas_call | solution.py:383
  36.5 0.9 %shard_map.86 = (bf16[1,1,256,1024]{3,2,1,0:T(8,128)(2,1)}, bf16[1,1,256,256]{3,2,1,0:T(8,128)(2,1)}, bf16[1,128,256]{2,1,0:T(8,128)(2,1)}) custom-call(bf16[1,1,256,1024]{3,2,1,0:T(8,128)(2,1)S(1)} %get-tuple-element.6.refs_0_, bf16[1,1,256,256]{3,2,1,0:T(8,128)(2,1)S(1)} %get-tuple-element.7.refs_1_, bf16[1,128,256]{2,1,0:T(8,128)(2,1)S(1)} %get-tuple-element.8.refs_2_), custom_call_target="tpu_custom_call" | custom-call | tf_op jit(solution)/shard_map/pallas_call | solution.py:425

commit v2 on v1

--- a/solution.py
+++ b/solution.py
@@ -17,8 +17,8 @@
 SUB = 64
 SUBS = CHUNK // SUB
 
-ORDER = [(1, 0), (0, 0), (0, 1), (2, 0), (0, 3), (3, 0), (3, 3), (1, 1),
-         (2, 3), (1, 3), (0, 2), (2, 1), (3, 1), (3, 2), (1, 2), (2, 2)]
+ORDER = [(0, 0), (3, 0), (0, 3), (1, 0), (0, 1), (2, 0), (3, 1), (3, 3), (0, 2), (1, 1), (3, 2), (1, 3), (2, 3), (2,
+    1), (1, 2), (2, 2)]
 SLOT = {off: i + 2 for i, off in enumerate(ORDER)}
 PLACE = {off: i for i, off in enumerate(off for off in ORDER if off != (0, 0))}
 CHUNKS = (len(ORDER) + 2) // 2
@@ -28,18 +28,22 @@
     return ((off[0] - way[0]) % SIDE, (off[1] - way[1]) % SIDE)
 
 
-GATHER = [((0, 0), (far, 0)) for far in (1, -1, 2)]
-for i in (1, 0, 3, 2):
-    way = 1 if i % 2 == 0 else -1
-    GATHER += [((i, 0), (0, way)), ((i, 0), (0, -way)), ((i, -way % SIDE), (0, way))]
+GATHER = [((0, 3), (0, 1)), ((0, 3), (-1, 0)), ((3, 0), (0, -1)), ((0, 0), (1, 0)), ((3, 0), (0, 1)), ((1, 0), (0,
+    2)), ((2, 0), (0, 1)), ((2, 0), (0, -1)), ((0, 0), (0, -1)), ((0, 0), (0, 1)), ((0, 0), (-1, 0)), ((3, 2), (1,
+    0)), ((0, 0), (2, 0)), ((3, 0), (0, 2)), ((0, 1), (-1, 0))]
+SUMS = [((3, 0), (0, 1)), ((1, 0), (0, 1)), ((0, 0), (2, 0)), ((0, 0), (0, -1)), ((3, 0), (0, 2)), ((0, 0), (0, 1)),
+    ((2, 0), (0, -1)), ((0, 0), (0, 2)), ((1, 0), (0, -1)), ((0, 0), (1, 0)), ((3, 0), (0, -1)), ((0, 0), (-1, 0)),
+    ((2, 0), (0, 2)), ((1, 0), (0, 2)), ((2, 0), (0, 1))]
 LANDS = {shifted(*move): move for move in GATHER}
-REDUCE = {to: tuple(step if step == 2 else -step for step in way) for to, (_, way) in LANDS.items()}
+REDUCE = {shifted(*move): tuple(step if step == 2 else -step for step in move[1]) for move in SUMS}
 TERMS = {off: [o for o in ORDER if o in REDUCE and shifted(o, REDUCE[o]) == off] for off in ORDER}
 
-ARRIVALS = [[], [(3, 0), (1, 0)], [(0, 1), (2, 0)], [(3, 1), (0, 3)], [(3, 3), (1, 1)], [(2, 3), (1, 3)], [(0, 2), (2, 1)],
-            [(1, 2), (3, 2)], [(2, 2)]]
-DEPARTURES = [[(2, 2), (1, 2)], [(3, 2)], [(2, 1), (0, 2)], [(1, 3), (2, 3)], [(3, 1), (1, 1), (3, 3)], [(0, 3)],
-              [(2, 0), (0, 1)], [(3, 0), (1, 0)], []]
+ARRIVALS = [[], [(3, 0)], [(0, 1), (0, 3), (1, 0)], [(2, 0)], [(3, 1), (3, 3)], [(3, 2), (0, 2), (1, 1)], [(1, 3)],
+    [(2, 3), (2, 1)], [(1, 2), (2, 2)]]
+DEPARTURES = [[(2, 2), (1, 2)], [(2, 1), (2, 3)], [(1, 3), (3, 2)], [(1, 1), (0, 2)], [(3, 3), (3, 1)], [(2, 0), (0,
+    1)], [(1, 0), (0, 3)], [(3, 0)], []]
+LATE = []
+LAST = DEPARTURES[-2] + DEPARTURES[-1] + LATE
 
 
 def dot(a, b):
@@ -60,7 +64,9 @@
         steps = [(place + step + SIDE) % SIDE - place for place, step in zip(places, way)]
         return (me_dp, me + steps[0] * strides[0] + steps[1] * strides[1])
 
-    near = {way: away(way) for way in dict.fromkeys([w for _, w in GATHER] + list(REDUCE.values()))}
+    ways = [way for _, way in GATHER + SUMS]
+    ways += [tuple(step if step == 2 else -step for step in way) for way in ways]
+    near = {way: away(way) for way in dict.fromkeys(ways)}
     sibling = (me_dp // 2 * 2 + (1 - me_dp % 2), me)
     above, below = ((me_dp + 2) % dp, me), ((me_dp + dp - 2) % dp, me)
     c2 = scale * math.log2(math.e)
@@ -322,6 +328,9 @@
                     for off in DEPARTURES[at]:
                         depart(off)
 
+    for off in LATE:
+        depart(off)
+
     @pl.when(core == 0)
     def _():
         total_back.wait_recv()
@@ -337,7 +346,7 @@
     for move in GATHER:
         ag_copy(move).wait_send()
     for off in REDUCE:
-        if off not in DEPARTURES[-2]:
+        if off not in LAST:
             rs_copy(off).wait_send()
 
     @pl.when(core == 0)
@@ -356,7 +365,7 @@
     total = summed((0, 0))
     p_out[0, :, 0:BLOCK] = (total[:, 0:BLOCK] * factor_root).astype(BF16)
     p_out[0, :, BLOCK : 2 * BLOCK] = (total[:, BLOCK : 2 * BLOCK] * factor).astype(BF16)
-    for off in DEPARTURES[-2]:
+    for off in LAST:
         rs_copy(off).wait_send()
 
 

time: 37.6 us -> 37 us (0.984); the launches traced: 37.4 us -> 36.4 us
  Pallas kernels: 35.5 us -> 34.5 us
    pallas_call x1, Pallas kernels: 34.6 us -> 33.6 us  [on_device(): pl.pallas_call(functools.partial(kernel, dp, heads, rows, 1.0 / BLOCK **...]
where the time goes in v2:
time: 37 us; the launch traced here: 36.4 us
  Pallas kernels  34.5 us (93%)
  between operations  1.93 us (5%)
    pallas_call x1, Pallas kernels, on_device(): pl.pallas_call(functools.partial(kernel, dp, heads, rows, 1.0 / BLOCK **...  33.6 us
    pallas_call x1, Pallas kernels, on_device(): pl.pallas_call(hand_over, out_shape=shapes, in_specs=[pl.BlockSpec(memory...  0.92 us

profile of v2, /device:TPU:1, one launch (start us, length us, event | category | flops | bytes accessed | tf_op | source)
XLA Modules:
  0.0 36.4 jit_solution(942144554593663988)
XLA Ops:
  1.9 33.6 %shard_map.85 = (bf16[1,1,256,1024]{3,2,1,0:T(8,128)(2,1)S(1)}, bf16[1,1,256,256]{3,2,1,0:T(8,128)(2,1)S(1)}, bf16[1,128,256]{2,1,0:T(8,128)(2,1)S(1)}) custom-call(bf16[1,1,256,1024]{3,2,1,0:T(8,128)(2,1)} %q_hbm.1, bf16[1,1,256,256]{3,2,1,0:T(8,128)(2,1)} %rkv_hbm.1, bf16[1,1,256,1024]{3,2,1,0:T(8,128)(2,1)} %g_hbm.1, bf16[1,128,256]{2,1,0:T(8,128)(2,1)} %pkv_hbm.1, ...), custom_call_target="tpu_custom_call" | custom-call | tf_op jit(solution)/shard_map/pallas_call | solution.py:392
  35.5 0.9 %shard_map.86 = (bf16[1,1,256,1024]{3,2,1,0:T(8,128)(2,1)}, bf16[1,1,256,256]{3,2,1,0:T(8,128)(2,1)}, bf16[1,128,256]{2,1,0:T(8,128)(2,1)}) custom-call(bf16[1,1,256,1024]{3,2,1,0:T(8,128)(2,1)S(1)} %get-tuple-element.6.refs_0_, bf16[1,1,256,256]{3,2,1,0:T(8,128)(2,1)S(1)} %get-tuple-element.7.refs_1_, bf16[1,128,256]{2,1,0:T(8,128)(2,1)S(1)} %get-tuple-element.8.refs_2_), custom_call_target="tpu_custom_call" | custom-call | tf_op jit(solution)/shard_map/pallas_call | solution.py:434

commit v3 on v2

--- a/solution.py
+++ b/solution.py
@@ -301,10 +301,12 @@
                 for i in range(SUBS):
                     span = slice(i * SUB, (i + 1) * SUB)
                     share = jnp.exp2((mh_ref[c, h, i] - mf_ref[h]) * c2) * inverse
-                    p = p_ref[c, h, span, :].astype(F32).reshape(SUB // 8, 8, rows) * share[None]
-                    ds = p * (dp_ref[c, h, span, :].reshape(p.shape) - row_dots[None])
-                    probs.append(p.reshape(SUB, rows).astype(BF16))
-                    dscores.append(ds.reshape(SUB, rows).astype(BF16))
+                    share = jnp.concatenate([share, share], axis=0).astype(BF16)
+                    p = (p_ref[c, h, span, :].reshape(SUB // 16, 16, rows) * share[None]).reshape(SUB, rows)
+                    ds = dp_ref[c, h, span, :].reshape(SUB // 8, 8, rows) - row_dots[None]
+                    ds = p.astype(F32) * ds.reshape(SUB, rows)
+                    probs.append(p)
+                    dscores.append(ds.astype(BF16))
                 probs2.append(jnp.concatenate(probs, axis=0))
                 dscores2.append(jnp.concatenate(dscores, axis=0))
                 dq_ref[h] = dq_ref[h] + dot(kt_ref[c], dscores2[-1])

time: 37 us -> 37 us (level)
  no operation moved by 1% of the time
where the time goes in v3:
time: 37 us; the launch traced here: 36.5 us
  Pallas kernels  34.5 us (93%)
  between operations  1.93 us (5%)
    pallas_call x1, Pallas kernels, on_device(): pl.pallas_call(functools.partial(kernel, dp, heads, rows, 1.0 / BLOCK **...  33.6 us
    pallas_call x1, Pallas kernels, on_device(): pl.pallas_call(hand_over, out_shape=shapes, in_specs=[pl.BlockSpec(memory...  0.92 us

profile of v3, /device:TPU:1, one launch (start us, length us, event | category | flops | bytes accessed | tf_op | source)
XLA Modules:
  0.0 36.5 jit_solution(7099100524779593788)
XLA Ops:
  1.9 33.6 %shard_map.85 = (bf16[1,1,256,1024]{3,2,1,0:T(8,128)(2,1)S(1)}, bf16[1,1,256,256]{3,2,1,0:T(8,128)(2,1)S(1)}, bf16[1,128,256]{2,1,0:T(8,128)(2,1)S(1)}) custom-call(bf16[1,1,256,1024]{3,2,1,0:T(8,128)(2,1)} %q_hbm.1, bf16[1,1,256,256]{3,2,1,0:T(8,128)(2,1)} %rkv_hbm.1, bf16[1,1,256,1024]{3,2,1,0:T(8,128)(2,1)} %g_hbm.1, bf16[1,128,256]{2,1,0:T(8,128)(2,1)} %pkv_hbm.1, ...), custom_call_target="tpu_custom_call" | custom-call | tf_op jit(solution)/shard_map/pallas_call | solution.py:394
  35.5 0.9 %shard_map.86 = (bf16[1,1,256,1024]{3,2,1,0:T(8,128)(2,1)}, bf16[1,1,256,256]{3,2,1,0:T(8,128)(2,1)}, bf16[1,128,256]{2,1,0:T(8,128)(2,1)}) custom-call(bf16[1,1,256,1024]{3,2,1,0:T(8,128)(2,1)S(1)} %get-tuple-element.6.refs_0_, bf16[1,1,256,256]{3,2,1,0:T(8,128)(2,1)S(1)} %get-tuple-element.7.refs_1_, bf16[1,128,256]{2,1,0:T(8,128)(2,1)S(1)} %get-tuple-element.8.refs_2_), custom_call_target="tpu_custom_call" | custom-call | tf_op jit(solution)/shard_map/pallas_call | solution.py:436

commit v4 on v2

--- a/solution.py
+++ b/solution.py
@@ -44,6 +44,18 @@
     1)], [(1, 0), (0, 3)], [(3, 0)], []]
 LATE = []
 LAST = DEPARTURES[-2] + DEPARTURES[-1] + LATE
+
+
+def choose(index, low, actions):
+    if len(actions) == 1:
+        actions[0]()
+        return
+    half = len(actions) // 2
+    lax.cond(
+        index < low + half,
+        lambda: choose(index, low, actions[:half]),
+        lambda: choose(index, low + half, actions[half:]),
+    )
 
 
 def dot(a, b):
@@ -240,17 +252,15 @@
 
     @pl.loop(1, CHUNKS)
     def _(c):
-        for chunk in range(1, CHUNKS):
-            @pl.when(c == chunk)
-            def _():
-                for off in ARRIVALS[chunk]:
-                    arrive(off)
-
-        for i in range(4):
-            @pl.when((c == 2 * i + 1) & (core == 1))
-            def _():
-                mask_step(i)
-
+        def before(chunk):
+            for off in ARRIVALS[chunk]:
+                arrive(off)
+            if chunk in (1, 3, 5, 7):
+                @pl.when(core == 1)
+                def _():
+                    mask_step(chunk // 2)
+
+        choose(c, 1, [functools.partial(before, chunk) for chunk in range(1, CHUNKS)])
         keys, values = chunk_kv(c)
         for h in range(heads):
             forward_head(c, h, keys, values, None)
@@ -316,17 +326,17 @@
         span = pl.ds(pl.multiple_of(c * CHUNK, CHUNK), CHUNK)
         part_ref[span, 0:BLOCK] = k_total.astype(BF16)
         part_ref[span, BLOCK : 2 * BLOCK] = v_total.astype(BF16)
-        for i in range(4, most + 1):
-            @pl.when((step == 2 * (i - 4)) & (core == 1))
-            def _():
-                mask_step(i)
-
-        for at in range(CHUNKS):
-            if DEPARTURES[at]:
-                @pl.when(step == at)
+
+        def after(at):
+            if at % 2 == 0 and 4 + at // 2 <= most:
+                @pl.when(core == 1)
                 def _():
-                    for off in DEPARTURES[at]:
-                        depart(off)
+                    mask_step(4 + at // 2)
+
+            for off in DEPARTURES[at]:
+                depart(off)
+
+        choose(step, 0, [functools.partial(after, at) for at in range(CHUNKS)])
 
     for off in LATE:
         depart(off)

time: 37 us -> 36.6 us (0.989); the launches traced: 36.4 us -> 36.5 us
  no operation moved by 1% of the time
where the time goes in v4:
time: 36.6 us; the launch traced here: 36.5 us
  Pallas kernels  34.5 us (94%)
  between operations  1.93 us (5%)
    pallas_call x1, Pallas kernels, on_device(): pl.pallas_call(functools.partial(kernel, dp, heads, rows, 1.0 / BLOCK **...  33.6 us
    pallas_call x1, Pallas kernels, on_device(): pl.pallas_call(hand_over, out_shape=shapes, in_specs=[pl.BlockSpec(memory...  0.92 us

profile of v4, /device:TPU:1, one launch (start us, length us, event | category | flops | bytes accessed | tf_op | source)
XLA Modules:
  0.0 36.5 jit_solution(4704264805509832624)
XLA Ops:
  1.9 33.6 %shard_map.85 = (bf16[1,1,256,1024]{3,2,1,0:T(8,128)(2,1)S(1)}, bf16[1,1,256,256]{3,2,1,0:T(8,128)(2,1)S(1)}, bf16[1,128,256]{2,1,0:T(8,128)(2,1)S(1)}) custom-call(bf16[1,1,256,1024]{3,2,1,0:T(8,128)(2,1)} %q_hbm.1, bf16[1,1,256,256]{3,2,1,0:T(8,128)(2,1)} %rkv_hbm.1, bf16[1,1,256,1024]{3,2,1,0:T(8,128)(2,1)} %g_hbm.1, bf16[1,128,256]{2,1,0:T(8,128)(2,1)} %pkv_hbm.1, ...), custom_call_target="tpu_custom_call" | custom-call | tf_op jit(solution)/shard_map/pallas_call | solution.py:402
  35.5 0.9 %shard_map.86 = (bf16[1,1,256,1024]{3,2,1,0:T(8,128)(2,1)}, bf16[1,1,256,256]{3,2,1,0:T(8,128)(2,1)}, bf16[1,128,256]{2,1,0:T(8,128)(2,1)}) custom-call(bf16[1,1,256,1024]{3,2,1,0:T(8,128)(2,1)S(1)} %get-tuple-element.6.refs_0_, bf16[1,1,256,256]{3,2,1,0:T(8,128)(2,1)S(1)} %get-tuple-element.7.refs_1_, bf16[1,128,256]{2,1,0:T(8,128)(2,1)S(1)} %get-tuple-element.8.refs_2_), custom_call_target="tpu_custom_call" | custom-call | tf_op jit(solution)/shard_map/pallas_call | solution.py:444
